TPU v7x, 32 devices: a whole 2x2x4 slice. The times are simulated.
32 devices in a mesh: basin: 2 (over y), row: 4 (over z), col: 4 (over x, core).
Axes of the slice: x: 2, y: 2, z: 4, core: 2. Of those that a mesh axis runs over, the one named last changes fastest.
Arguments:
- wet_mask: int32 [512, 4096], P(('basin', 'row'), 'col'), parts along dimension 0, may hold values 0 or 1
- land_class: int32 [512, 4096], P(('basin', 'row'), 'col'), parts along dimension 0, may hold values from 0 to 15
- flood_label: int32 [512, 4096], P(('basin', 'row'), 'col'), parts along dimension 0, may hold values 0 or 1
- conductance: float32 [16], replicated, may hold values from 0.5 to 3
- storage: float32 [512, 4096], P(('basin', 'row'), 'col'), parts along dimension 0, may hold values from 0.1 to 1
- prior_depth: float32 [512, 4096], P(('basin', 'row'), 'col'), parts along dimension 0, may hold values from -6 to 6
- rainfall: float32 [512, 4096], P(('basin', 'row'), 'col'), parts along dimension 0, may hold values from -6 to 6
Outputs:
- depth_iterate: float32 [512, 4096], P(('basin', 'row'), 'col'), parts along dimension 0
- adjoint_iterate: float32 [512, 4096], P(('basin', 'row'), 'col'), parts along dimension 0
There are 2 independent parts, one for each index of `basin`. A program takes and returns all parts, laid end to end along the dimension named above; an argument that names none is the same for every part. Nothing has to cross between parts.
All inputs are finite; a program needn't handle non-finite values. No bound on the sum of `wet_mask` or of `flood_label` on one device may be relied on, other than what follows from the above.
Results may differ from a plain program's by a relative error of at most 0.00015.
Values sent between devices are 32-bit elements; how exact they have to be, the bound alone decides.
A program may use at most 64 MiB of HBM per device.

v0:
```python
import jax
import jax.numpy as jnp
from jax import lax
from jax.sharding import PartitionSpec as P

ITERS = 3


def extended(value, sides, width):
    for axis, dim in sides:
        devices, length = (lax.axis_size(axis), value.shape[dim])
        up = [(i, (i + 1) % devices) for i in range(devices - 1)]
        down = [(j, i) for i, j in up]
        last = lax.slice_in_dim(value, length - width, length, axis=dim)
        initial = lax.slice_in_dim(value, 0, width, axis=dim)
        before = lax.ppermute(last, axis, up)
        after = lax.ppermute(initial, axis, down)
        value = jnp.concatenate([before, value, after], axis=dim)
    return value


def cell_values(wet, land_class, conductance):
    value = jnp.zeros(land_class.shape, jnp.float32)
    for level in range(conductance.shape[0]):
        value = value + jnp.where(land_class == level, conductance[level], 0.0)
    return value * wet


def build_operator(cell, storage):
    padded = extended(cell, (("row", 0), ("col", 1)), 1)
    k_up = cell * padded[:-2, 1:-1]
    k_down = cell * padded[2:, 1:-1]
    k_left = cell * padded[1:-1, :-2]
    k_right = cell * padded[1:-1, 2:]
    diagonal = storage + k_up + k_down + k_left + k_right
    return (diagonal, k_up, k_down, k_left, k_right)


def margin(stacked, width):
    return extended(stacked, (("row", 1), ("col", 2)), width)


def apply_padded(padded, field, coeffs):
    diagonal, k_up, k_down, k_left, k_right = coeffs
    return (
        diagonal * field
        - k_up * padded[:, :-2, 1:-1]
        - k_down * padded[:, 2:, 1:-1]
        - k_left * padded[:, 1:-1, :-2]
        - k_right * padded[:, 1:-1, 2:]
    )


def operate(field, coeffs):
    return apply_padded(margin(field, 1), field, coeffs)


def squares(residual):
    return lax.psum(jnp.sum(residual * residual, axis=(1, 2)), ("row", "col"))


def widen(scalars):
    return scalars[:, None, None]


def body(wet_mask, land_class, flood_label, conductance, storage, prior_depth, rainfall):
    wet = wet_mask.astype(jnp.float32)
    cell = cell_values(wet, land_class, conductance)
    coeffs = build_operator(cell, storage)
    forward_side = storage * prior_depth + wet * rainfall
    adjoint_side = wet * (jax.nn.sigmoid(prior_depth) - flood_label.astype(jnp.float32))
    right = jnp.stack([forward_side, adjoint_side])
    solution = jnp.zeros_like(right)
    residual = right
    direction = right
    norm_now = squares(residual)
    for step in range(ITERS):
        image = operate(direction, coeffs)
        curve = lax.psum(jnp.sum(direction * image, axis=(1, 2)), ("row", "col"))
        alpha = norm_now / curve
        solution = solution + widen(alpha) * direction
        residual = residual - widen(alpha) * image
        norm_next = squares(residual)
        direction = residual + widen(norm_next / norm_now) * direction
        norm_now = norm_next
    return (solution[0], solution[1])


def solution(mesh):
    return jax.shard_map(
        body,
        mesh=mesh,
        in_specs=(
            P(("basin", "row"), "col"),
            P(("basin", "row"), "col"),
            P(("basin", "row"), "col"),
            P(),
            P(("basin", "row"), "col"),
            P(("basin", "row"), "col"),
            P(("basin", "row"), "col"),
        ),
        out_specs=(P(("basin", "row"), "col"), P(("basin", "row"), "col")),
        check_vma=False,
    )
```

profile of v0, /device:TPU:0, one launch (start us, length us, event | category | flops | bytes accessed | tf_op | source)
XLA Modules:
  0.0 228.0 jit_solution(12439779417905594402)
XLA Ops:
  0.6 1.9 fusion.41
  2.6 11.5 %add_multiply_fusion = f32[64,1024]{1,0:T(8,128)S(1)} fusion(s32[64,1024]{1,0:T(8,128)} %param.7, s32[64,1024]{1,0:T(8,128)} %param.8, f32[]{:T(128)} %bitcast.17, f32[]{:T(128)} %bitcast.16, f32[]{:T(128)} %bitcast.15, f32[]{:T(128)} %bitcast.14, f32[]{:T(128)} %bitcast.13, f32[]{:T(128)} %bitcast.12, f32[]{:T(128)} %bitcast.11, f32[]{:T(128)} %bitcast.10, ...), kind=kLoop, calls=%fused_computation.84 | loop fusion | flops 3211264 | bytes 786496 | tf_op jit(solution)/shard_map/mul | solution.py:26
  14.1 1.4 collective-permute-start.1
  15.5 5.6 %collective-permute-start = (f32[1,1024]{1,0:T(1,128)S(1)}, f32[1,1024]{1,0:T(1,128)S(1)}, u32[]{:S(2)}, u32[]{:S(2)}) collective-permute-start(f32[1,1024]{1,0:T(1,128)S(1)} %get-tuple-element.37), channel_id=1, source_target_pairs={{0,4},{4,8},{8,12},{1,5},{5,9},{9,13},{2,6},{6,10},{10,14},{3,7},{... | collective-permute-start | bytes 12296 | tf_op jit(solution)/shard_map/ppermute | solution.py:16
  21.1 1.3 collective-permute-done
  22.4 0.1 pad_maximum_fusion.47
  22.5 1.3 collective-permute-start.3
  23.8 3.0 %collective-permute-start.2 = (f32[66,1]{1,0:T(8,128)S(1)}, f32[66,1]{1,0:T(8,128)S(1)}, u32[]{:S(2)}, u32[]{:S(2)}) collective-permute-start(f32[66,1]{1,0:T(8,128)S(1)} %get-tuple-element.33), channel_id=1, source_target_pairs={{0,1},{1,2},{2,3},{4,5},{5,6},{6,7},{8,9},{9,10},{10,11},{12,13},{... | collective-permute-start | bytes 800 | tf_op jit(solution)/shard_map/ppermute | solution.py:16
  26.9 0.8 collective-permute-done.2
  27.7 1.3 add_add_fusion
  29.0 4.2 %collective-permute-start.4 = (f32[2,1,1024]{2,1,0:T(1,128)S(1)}, f32[2,1,1024]{2,1,0:T(1,128)S(1)}, u32[]{:S(2)}, u32[]{:S(2)}) collective-permute-start(f32[2,1,1024]{2,1,0:T(1,128)S(1)} %get-tuple-element.28), channel_id=1, source_target_pairs={{0,4},{4,8},{8,12},{1,5},{5,9},{9,13},{2,6},{6,10},{10,14},{3,7},{... | collective-permute-start | bytes 24584 | tf_op jit(solution)/shard_map/ppermute | solution.py:16
  33.2 1.3 collective-permute-start.5
  34.5 0.0 collective-permute-done.4
  34.5 4.2 %collective-permute-done.5 = f32[2,1,1024]{2,1,0:T(1,128)S(1)} collective-permute-done((f32[2,1,1024]{2,1,0:T(1,128)S(1)}, f32[2,1,1024]{2,1,0:T(1,128)S(1)}, u32[]{:S(2)}, u32[]{:S(2)}) %collective-permute-start.5) | collective-permute-done | bytes 8224 | tf_op jit(solution)/shard_map/ppermute | solution.py:17
  38.7 0.1 pad_maximum_fusion.46
  38.8 2.2 collective-permute-start.6
  41.1 1.3 collective-permute-start.7
  42.4 5.1 %collective-permute-done.7 = f32[2,66,1]{2,1,0:T(8,128)S(1)} collective-permute-done((f32[2,66,1]{2,1,0:T(8,128)S(1)}, f32[2,66,1]{2,1,0:T(8,128)S(1)}, u32[]{:S(2)}, u32[]{:S(2)}) %collective-permute-start.7) | collective-permute-done | bytes 560 | tf_op jit(solution)/shard_map/ppermute | solution.py:17
  47.5 0.5 multiply_reduce_fusion.3
  48.0 32.5 %all-reduce = (f32[2]{0:T(128)S(1)}, f32[2]{0:T(128)S(1)}) all-reduce(f32[2]{0:T(128)S(1)} %get-tuple-element.3, f32[2]{0:T(128)S(1)} %get-tuple-element.2), channel_id=1, replica_groups=mesh['basin'=2,'row'=4,'col'=4] {'row','col'}, use_global_device_ids=true, to_apply=%region_1.2 | all-reduce | flops 4 | bytes 32 | tf_op jit(solution)/shard_map/psum | solution.py:59
  80.5 0.3 multiply_reduce_fusion.2
  80.8 29.5 %psum.44 = f32[2]{0:T(128)S(1)} all-reduce(f32[2]{0:T(128)S(1)} %get-tuple-element.8), channel_id=1, replica_groups=mesh['basin'=2,'row'=4,'col'=4] {'row','col'}, use_global_device_ids=true, to_apply=%region_5.6 | all-reduce | flops 2 | bytes 16 | tf_op jit(solution)/shard_map/psum | solution.py:59
  110.2 0.1 multiply_add_fusion.2
  110.4 1.3 collective-permute-start.8
  111.7 1.3 collective-permute-start.9
  113.0 0.0 collective-permute-done.8
  113.1 4.2 %collective-permute-done.9 = f32[2,1,1024]{2,1,0:T(1,128)S(1)} collective-permute-done((f32[2,1,1024]{2,1,0:T(1,128)S(1)}, f32[2,1,1024]{2,1,0:T(1,128)S(1)}, u32[]{:S(2)}, u32[]{:S(2)}) %collective-permute-start.9) | collective-permute-done | bytes 8224 | tf_op jit(solution)/shard_map/ppermute | solution.py:17
  117.3 0.1 pad_maximum_fusion.42
  117.4 1.3 collective-permute-start.10
  118.7 1.3 collective-permute-start.11
  120.0 1.8 collective-permute-done.11
  121.8 0.6 multiply_reduce_fusion.1
  122.4 31.3 %psum.45 = f32[2]{0:T(128)S(1)} all-reduce(f32[2]{0:T(128)S(1)} %get-tuple-element.6), channel_id=1, replica_groups=mesh['basin'=2,'row'=4,'col'=4] {'row','col'}, use_global_device_ids=true, to_apply=%region_7.8 | all-reduce | flops 2 | bytes 16 | tf_op jit(solution)/shard_map/psum | solution.py:79
  153.7 0.3 multiply_reduce_fusion
  154.0 29.5 %psum.46 = f32[2]{0:T(128)S(1)} all-reduce(f32[2]{0:T(128)S(1)} %multiply_reduce_fusion), channel_id=1, replica_groups=mesh['basin'=2,'row'=4,'col'=4] {'row','col'}, use_global_device_ids=true, to_apply=%region_9.10 | all-reduce | flops 2 | bytes 16 | tf_op jit(solution)/shard_map/psum | solution.py:59
  183.5 0.2 multiply_add_fusion.1
  183.7 1.3 collective-permute-start.12
  185.0 1.3 collective-permute-start.13
  186.3 0.0 collective-permute-done.12
  186.4 4.2 %collective-permute-done.13 = f32[2,1,1024]{2,1,0:T(1,128)S(1)} collective-permute-done((f32[2,1,1024]{2,1,0:T(1,128)S(1)}, f32[2,1,1024]{2,1,0:T(1,128)S(1)}, u32[]{:S(2)}, u32[]{:S(2)}) %collective-permute-start.13) | collective-permute-done | bytes 8224 | tf_op jit(solution)/shard_map/ppermute | solution.py:17
  190.6 0.1 pad_maximum_fusion.39
  190.7 1.3 collective-permute-start.14
  192.0 1.3 collective-permute-start.15
  193.3 1.8 collective-permute-done.15
  195.1 0.5 fusion.3
  195.7 31.3 %psum.47 = f32[2]{0:T(128)S(1)} all-reduce(f32[2]{0:T(128)S(1)} %fusion.3), channel_id=1, replica_groups=mesh['basin'=2,'row'=4,'col'=4] {'row','col'}, use_global_device_ids=true, to_apply=%region_11.12 | all-reduce | flops 2 | bytes 16 | tf_op jit(solution)/shard_map/psum | solution.py:79
  227.0 0.2 multiply_add_fusion
  227.2 0.8 slice_bitcast_fusion
  (22 shorter events, 0.1 us)
Async XLA Ops:
  2.6 25.1 %copy-start.1 = (f32[64,1024]{1,0:T(8,128)S(1)}, f32[64,1024]{1,0:T(8,128)}, u32[]{:S(2)}) copy-start(f32[64,1024]{1,0:T(8,128)} %param.11) | copy-start | bytes 786436
  2.6 25.1 %copy-start.2 = (s32[64,1024]{1,0:T(8,128)S(1)}, s32[64,1024]{1,0:T(8,128)}, u32[]{:S(2)}) copy-start(s32[64,1024]{1,0:T(8,128)} %param.9) | copy-start | bytes 786436
  2.6 25.1 %copy-start.3 = (f32[64,1024]{1,0:T(8,128)S(1)}, f32[64,1024]{1,0:T(8,128)}, u32[]{:S(2)}) copy-start(f32[64,1024]{1,0:T(8,128)} %param.12) | copy-start | bytes 786436
  14.1 13.6 %copy-start = (s32[64,1024]{1,0:T(8,128)S(1)}, s32[64,1024]{1,0:T(8,128)}, u32[]{:S(2)}) copy-start(s32[64,1024]{1,0:T(8,128)} %param.7) | copy-start | bytes 786436
  14.1 7.0 %collective-permute-start.1 = (f32[1,1024]{1,0:T(1,128)S(1)}, f32[1,1024]{1,0:T(1,128)S(1)}, u32[]{:S(2)}, u32[]{:S(2)}) collective-permute-start(f32[1,1024]{1,0:T(1,128)S(1)} %get-tuple-element.36), channel_id=1, source_target_pairs={{4,0},{8,4},{12,8},{5,1},{9,5},{13,9},{6,2},{10,6},{14,10},{7,3},{... | collective-permute-start | bytes 12296 | tf_op jit(solution)/shard_map/ppermute | solution.py:17
  15.5 6.9 %collective-permute-start = (f32[1,1024]{1,0:T(1,128)S(1)}, f32[1,1024]{1,0:T(1,128)S(1)}, u32[]{:S(2)}, u32[]{:S(2)}) collective-permute-start(f32[1,1024]{1,0:T(1,128)S(1)} %get-tuple-element.37), channel_id=1, source_target_pairs={{0,4},{4,8},{8,12},{1,5},{5,9},{9,13},{2,6},{6,10},{10,14},{3,7},{... | collective-permute-start | bytes 12296 | tf_op jit(solution)/shard_map/ppermute | solution.py:16
  22.5 4.3 %collective-permute-start.3 = (f32[66,1]{1,0:T(8,128)S(1)}, f32[66,1]{1,0:T(8,128)S(1)}, u32[]{:S(2)}, u32[]{:S(2)}) collective-permute-start(f32[66,1]{1,0:T(8,128)S(1)} %get-tuple-element.32), channel_id=1, source_target_pairs={{1,0},{2,1},{3,2},{5,4},{6,5},{7,6},{9,8},{10,9},{11,10},{13,12},{... | collective-permute-start | bytes 800 | tf_op jit(solution)/shard_map/ppermute | solution.py:17
  23.8 3.9 %collective-permute-start.2 = (f32[66,1]{1,0:T(8,128)S(1)}, f32[66,1]{1,0:T(8,128)S(1)}, u32[]{:S(2)}, u32[]{:S(2)}) collective-permute-start(f32[66,1]{1,0:T(8,128)S(1)} %get-tuple-element.33), channel_id=1, source_target_pairs={{0,1},{1,2},{2,3},{4,5},{5,6},{6,7},{8,9},{9,10},{10,11},{12,13},{... | collective-permute-start | bytes 800 | tf_op jit(solution)/shard_map/ppermute | solution.py:16
  29.0 5.5 %collective-permute-start.4 = (f32[2,1,1024]{2,1,0:T(1,128)S(1)}, f32[2,1,1024]{2,1,0:T(1,128)S(1)}, u32[]{:S(2)}, u32[]{:S(2)}) collective-permute-start(f32[2,1,1024]{2,1,0:T(1,128)S(1)} %get-tuple-element.28), channel_id=1, source_target_pairs={{0,4},{4,8},{8,12},{1,5},{5,9},{9,13},{2,6},{6,10},{10,14},{3,7},{... | collective-permute-start | bytes 24584 | tf_op jit(solution)/shard_map/ppermute | solution.py:16
  33.2 5.5 %collective-permute-start.5 = (f32[2,1,1024]{2,1,0:T(1,128)S(1)}, f32[2,1,1024]{2,1,0:T(1,128)S(1)}, u32[]{:S(2)}, u32[]{:S(2)}) collective-permute-start(f32[2,1,1024]{2,1,0:T(1,128)S(1)} %get-tuple-element.29), channel_id=1, source_target_pairs={{4,0},{8,4},{12,8},{5,1},{9,5},{13,9},{6,2},{10,6},{14,10},{7,3},{... | collective-permute-start | bytes 24584 | tf_op jit(solution)/shard_map/ppermute | solution.py:17
  38.8 3.5 %collective-permute-start.6 = (f32[2,66,1]{2,1,0:T(8,128)S(1)}, f32[2,66,1]{2,1,0:T(8,128)S(1)}, u32[]{:S(2)}, u32[]{:S(2)}) collective-permute-start(f32[2,66,1]{2,1,0:T(8,128)S(1)} %get-tuple-element.20), channel_id=1, source_target_pairs={{0,1},{1,2},{2,3},{4,5},{5,6},{6,7},{8,9},{9,10},{10,11},{12,13},{... | collective-permute-start | bytes 1592 | tf_op jit(solution)/shard_map/ppermute | solution.py:16
  41.1 6.4 %collective-permute-start.7 = (f32[2,66,1]{2,1,0:T(8,128)S(1)}, f32[2,66,1]{2,1,0:T(8,128)S(1)}, u32[]{:S(2)}, u32[]{:S(2)}) collective-permute-start(f32[2,66,1]{2,1,0:T(8,128)S(1)} %get-tuple-element.21), channel_id=1, source_target_pairs={{1,0},{2,1},{3,2},{5,4},{6,5},{7,6},{9,8},{10,9},{11,10},{13,12},{... | collective-permute-start | bytes 1592 | tf_op jit(solution)/shard_map/ppermute | solution.py:17
  110.4 2.6 %collective-permute-start.8 = (f32[2,1,1024]{2,1,0:T(1,128)S(1)}, f32[2,1,1024]{2,1,0:T(1,128)S(1)}, u32[]{:S(2)}, u32[]{:S(2)}) collective-permute-start(f32[2,1,1024]{2,1,0:T(1,128)S(1)} %get-tuple-element.26), channel_id=1, source_target_pairs={{0,4},{4,8},{8,12},{1,5},{5,9},{9,13},{2,6},{6,10},{10,14},{3,7},{... | collective-permute-start | bytes 24584 | tf_op jit(solution)/shard_map/ppermute | solution.py:16
  111.7 5.5 %collective-permute-start.9 = (f32[2,1,1024]{2,1,0:T(1,128)S(1)}, f32[2,1,1024]{2,1,0:T(1,128)S(1)}, u32[]{:S(2)}, u32[]{:S(2)}) collective-permute-start(f32[2,1,1024]{2,1,0:T(1,128)S(1)} %get-tuple-element.27), channel_id=1, source_target_pairs={{4,0},{8,4},{12,8},{5,1},{9,5},{13,9},{6,2},{10,6},{14,10},{7,3},{... | collective-permute-start | bytes 24584 | tf_op jit(solution)/shard_map/ppermute | solution.py:17
  117.4 2.6 %collective-permute-start.10 = (f32[2,66,1]{2,1,0:T(8,128)S(1)}, f32[2,66,1]{2,1,0:T(8,128)S(1)}, u32[]{:S(2)}, u32[]{:S(2)}) collective-permute-start(f32[2,66,1]{2,1,0:T(8,128)S(1)} %get-tuple-element.18), channel_id=1, source_target_pairs={{0,1},{1,2},{2,3},{4,5},{5,6},{6,7},{8,9},{9,10},{10,11},{12,13},{... | collective-permute-start | bytes 1592 | tf_op jit(solution)/shard_map/ppermute | solution.py:16
  118.7 3.2 %collective-permute-start.11 = (f32[2,66,1]{2,1,0:T(8,128)S(1)}, f32[2,66,1]{2,1,0:T(8,128)S(1)}, u32[]{:S(2)}, u32[]{:S(2)}) collective-permute-start(f32[2,66,1]{2,1,0:T(8,128)S(1)} %get-tuple-element.19), channel_id=1, source_target_pairs={{1,0},{2,1},{3,2},{5,4},{6,5},{7,6},{9,8},{10,9},{11,10},{13,12},{... | collective-permute-start | bytes 1592 | tf_op jit(solution)/shard_map/ppermute | solution.py:17
  183.7 2.6 %collective-permute-start.12 = (f32[2,1,1024]{2,1,0:T(1,128)S(1)}, f32[2,1,1024]{2,1,0:T(1,128)S(1)}, u32[]{:S(2)}, u32[]{:S(2)}) collective-permute-start(f32[2,1,1024]{2,1,0:T(1,128)S(1)} %get-tuple-element.24), channel_id=1, source_target_pairs={{0,4},{4,8},{8,12},{1,5},{5,9},{9,13},{2,6},{6,10},{10,14},{3,7},{... | collective-permute-start | bytes 24584 | tf_op jit(solution)/shard_map/ppermute | solution.py:16
  185.0 5.5 %collective-permute-start.13 = (f32[2,1,1024]{2,1,0:T(1,128)S(1)}, f32[2,1,1024]{2,1,0:T(1,128)S(1)}, u32[]{:S(2)}, u32[]{:S(2)}) collective-permute-start(f32[2,1,1024]{2,1,0:T(1,128)S(1)} %get-tuple-element.25), channel_id=1, source_target_pairs={{4,0},{8,4},{12,8},{5,1},{9,5},{13,9},{6,2},{10,6},{14,10},{7,3},{... | collective-permute-start | bytes 24584 | tf_op jit(solution)/shard_map/ppermute | solution.py:17
  190.7 2.6 %collective-permute-start.14 = (f32[2,66,1]{2,1,0:T(8,128)S(1)}, f32[2,66,1]{2,1,0:T(8,128)S(1)}, u32[]{:S(2)}, u32[]{:S(2)}) collective-permute-start(f32[2,66,1]{2,1,0:T(8,128)S(1)} %get-tuple-element.16), channel_id=1, source_target_pairs={{0,1},{1,2},{2,3},{4,5},{5,6},{6,7},{8,9},{9,10},{10,11},{12,13},{... | collective-permute-start | bytes 1592 | tf_op jit(solution)/shard_map/ppermute | solution.py:16
  192.0 3.2 %collective-permute-start.15 = (f32[2,66,1]{2,1,0:T(8,128)S(1)}, f32[2,66,1]{2,1,0:T(8,128)S(1)}, u32[]{:S(2)}, u32[]{:S(2)}) collective-permute-start(f32[2,66,1]{2,1,0:T(8,128)S(1)} %get-tuple-element.17), channel_id=1, source_target_pairs={{1,0},{2,1},{3,2},{5,4},{6,5},{7,6},{9,8},{10,9},{11,10},{13,12},{... | collective-permute-start | bytes 1592 | tf_op jit(solution)/shard_map/ppermute | solution.py:17
where the time goes:
time: 229 us; the launch traced here: 228 us
  blocking collectives  154 us (67%)
  starting transfers between devices  30.6 us (13%)
  waiting for transfers between devices  23.7 us (10%)
  other arithmetic  15.9 us (7%)
  local copies, waits for them, and re-layouts  2.85 us (1%)
    psum x3, blocking collectives, squares(): return lax.psum(jnp.sum(residual * residual, axis=(1, 2)), ('row', 'col'))  91.4 us
    psum x2, blocking collectives, body(): curve = lax.psum(jnp.sum(direction * image, axis=(1, 2)), ('row', 'col'))  62.6 us
    ppermute x8, waiting for transfers between devices, extended(): after = lax.ppermute(initial, axis, down)  21.4 us
    ppermute x8, starting transfers between devices, extended(): before = lax.ppermute(last, axis, up)  20.2 us
    mul x1, other arithmetic, cell_values(): return value * wet  11.5 us
    ppermute x8, starting transfers between devices, extended(): after = lax.ppermute(initial, axis, down)  10.5 us
  transfers between devices with their start and end apart: 16, of which 8 were waited for; matrix products, arithmetic and copies ran while one was open for 0% of the time, Pallas kernels for 0%

commit v1 on v0

v1 whole, which is shorter than its diff:
```python
import functools

import jax
import jax.numpy as jnp
from jax import lax
from jax.experimental import pallas as pl
from jax.experimental.pallas import tpu as pltpu
from jax.sharding import PartitionSpec as P

MESH = pl.DeviceIdType.MESH
LANES = 128
SUB = 8
PIECE = 4
STEPS = (
    (-1, 0), (1, 0), (0, -1), (0, 1), (-1, -1), (-1, 1), (1, -1), (1, 1),
)
OPPOSITE = (1, 0, 3, 2, 7, 6, 5, 4)


def lookup(index, table):
    values = [table[i] for i in range(table.shape[0])]
    bit = 1
    while len(values) > 1:
        odd = (index & bit) != 0
        values = [jnp.where(odd, values[i + 1], values[i]) for i in range(0, len(values), 2)]
        bit *= 2
    return values[0]


def iota(shape, dim):
    return lax.broadcasted_iota(jnp.int32, shape, dim)


def fold(values):
    rows, lanes = values.shape
    return values.reshape(rows // SUB, SUB, lanes).sum(axis=0)


def coefficients(m, c):
    n = [c * m[k] + m[k + 1] for k in range(5)]
    a0 = m[0] / n[0]
    r0, r1 = 1.0 - a0 * c, -a0
    rr1 = r0 * r0 * m[0] + 2.0 * r0 * r1 * m[1] + r1 * r1 * m[2]
    p0, p1 = r0 + rr1 / m[0], r1
    curve = p0 * p0 * n[0] + 2.0 * p0 * p1 * n[1] + p1 * p1 * n[2]
    a1 = rr1 / curve
    u0, u1 = a0 + a1 * p0, a1 * p1
    r0, r1, r2 = r0 - a1 * c * p0, r1 - a1 * (p0 + c * p1), -a1 * p1
    rr2 = (r0 * r0 * m[0] + 2.0 * r0 * r1 * m[1] + (r1 * r1 + 2.0 * r0 * r2) * m[2]
           + 2.0 * r1 * r2 * m[3] + r2 * r2 * m[4])
    beta = rr2 / rr1
    p0, p1, p2 = r0 + beta * p0, r1 + beta * p1, r2
    curve = (p0 * p0 * n[0] + 2.0 * p0 * p1 * n[1] + (p1 * p1 + 2.0 * p0 * p2) * n[2]
             + 2.0 * p1 * p2 * n[3] + p2 * p2 * n[4])
    a2 = rr2 / curve
    return u0 + a2 * p0, u1 + a2 * p1, a2 * p2


def kernel(
    nrow, ncol, stages,
    wet_h, land_h, label_h, cond, stor_h, prior_h, rain_h, out0_h, out1_h,
    wet_v, land_v, label_v, stor_v, prior_v, rain_v, out_v,
    v0, v1, v2, cell_s, diag_s,
    pack_rows, pack_cols, got_rows, got_cols, part, got_part,
    in_sem, out_sem, send_sem, recv_sem, psend_sem, precv_sem,
):
    rows, cols = stor_v.shape
    nb, npan = rows // SUB, cols // LANES
    row, col = lax.axis_index("row"), lax.axis_index("col")

    loads = [
        pltpu.make_async_copy(src, dst, in_sem.at[i])
        for i, (src, dst) in enumerate((
            (land_h, land_v), (wet_h, wet_v), (stor_h, stor_v),
            (prior_h, prior_v), (rain_h, rain_v), (label_h, label_v)))
    ]
    for load in loads:
        load.start()

    got_rows[...] = jnp.zeros_like(got_rows)
    got_cols[...] = jnp.zeros_like(got_cols)

    there = []
    for dr, dc in STEPS:
        ok = True
        for at, d, n in ((row, dr, nrow), (col, dc, ncol)):
            if d:
                here = (at > 0) if d < 0 else (at < n - 1)
                ok = here if ok is True else jnp.logical_and(ok, here)
        there.append(ok)

    def place(k):
        dr, dc = STEPS[k]
        return {"row": row + dr, "col": col + dc}

    def peer(stage, k):
        if stage == "both":
            at = lax.rem(row * ncol + col + k, nrow * ncol)
            return {"row": at // ncol, "col": lax.rem(at, ncol)}
        if stage == "col":
            return {"row": row, "col": lax.rem(col + k, ncol)}
        return {"row": lax.rem(row + k, nrow), "col": col}

    counts = {"both": nrow * ncol, "row": nrow, "col": ncol}
    barrier = pltpu.get_barrier_semaphore()
    expect = 0
    for stage in stages:
        for k in range(1, counts[stage]):
            pl.semaphore_signal(barrier, inc=1, device_id=peer(stage, k), device_id_type=MESH)
        expect += counts[stage] - 1
    if "both" not in stages:
        for k in range(4, 8):
            @pl.when(there[k])
            def _():
                pl.semaphore_signal(barrier, inc=1, device_id=place(k), device_id_type=MESH)
            expect = expect + there[k].astype(jnp.int32)

    shift = cond[0]
    for i in range(1, cond.shape[0]):
        shift = shift + cond[i]
    shift = shift * (2.0 / cond.shape[0])
    shift = shift * shift

    for load in loads:
        load.wait()
    for j in range(npan):
        at = pl.ds(j * LANES, LANES)
        wet = wet_v[:, at].astype(jnp.float32)
        prior = prior_v[:, at]
        stor = stor_v[:, at]
        core = pl.ds(0, rows)
        cell_s[j, core, :] = lookup(land_v[:, at], cond) * wet
        v0[0, j, core, :] = stor * prior + wet * rain_v[:, at]
        v0[1, j, core, :] = wet * (1.0 / (1.0 + jnp.exp(-prior)) - label_v[:, at].astype(jnp.float32))
        diag_s[j, core, :] = stor

    fields = (v0.at[0], v0.at[1], cell_s, diag_s)
    sub = iota((SUB, LANES), 0)
    lane = iota((SUB, LANES), 1)
    upper = sub < PIECE
    halves = lane < LANES // 2

    for pair in range(2):
        fa, fb = fields[2 * pair], fields[2 * pair + 1]
        for j in range(npan):
            top = pl.ds(0, SUB)
            bottom = pl.ds(rows - SUB, SUB)
            pack_rows[0, pair, j] = jnp.where(upper, fa[j, top, :], pltpu.roll(fb[j, top, :], PIECE, 0))
            pack_rows[1, pair, j] = jnp.where(upper, pltpu.roll(fa[j, bottom, :], PIECE, 0), fb[j, bottom, :])

    left = jnp.zeros((SUB, LANES), jnp.float32)
    right = jnp.zeros((SUB, LANES), jnp.float32)
    slot = lane // PIECE
    for f, field in enumerate(fields):
        for r in range(nb):
            k = f * nb + r
            block = pl.ds(r * SUB, SUB)
            left = jnp.where(slot == k, pltpu.roll(field[0, block, :], PIECE * k, 1), left)
            right = jnp.where(
                slot == k, pltpu.roll(field[npan - 1, block, :], (PIECE * k + PIECE) % LANES, 1), right)
    pack_cols[0] = left
    pack_cols[1] = right

    pl.semaphore_wait(barrier, expect)

    def halo(k, arriving):
        dr, dc = STEPS[k]
        to = k if arriving else OPPOSITE[k]
        if dc == 0:
            src, dst = pack_rows.at[k], got_rows.at[to]
        else:
            src, dst = pack_cols.at[(dc + 1) // 2], got_cols.at[to - 2]
        return pltpu.make_async_remote_copy(
            src_ref=src, dst_ref=dst, send_sem=send_sem.at[k], recv_sem=recv_sem.at[to],
            device_id=place(k), device_id_type=MESH)

    for k in range(8):
        @pl.when(there[k])
        def _():
            halo(k, False).start()
    for k in range(8):
        @pl.when(there[k])
        def _():
            halo(k, True).wait_recv()

    tail = pl.ds(rows, SUB)
    for f, field in enumerate(fields):
        pair, second = f // 2, f % 2
        for j in range(npan):
            after, before = got_rows[1, pair, j], got_rows[0, pair, j]
            if second:
                after = pltpu.roll(after, PIECE, 0)
            else:
                before = pltpu.roll(before, PIECE, 0)
            field[j, tail, :] = jnp.where(upper, after, before)

        def side(after, before, r):
            k = f * nb + r
            after = pltpu.roll(after, (LANES - PIECE * k) % LANES, 1)
            before = pltpu.roll(before, LANES - PIECE - PIECE * k, 1)
            return jnp.where(halves, after, before)

        for r in range(nb):
            field[npan, pl.ds(r * SUB, SUB), :] = side(got_cols[1], got_cols[0], r)
        field[npan, tail, :] = jnp.where(
            upper, side(got_cols[5], got_cols[4], 0), side(got_cols[3], got_cols[2], nb - 1))

    tall = rows + SUB
    first = iota((tall, LANES), 1) == 0
    last = iota((tall, LANES), 1) == LANES - 1

    def around(panels):
        total = npan + 1
        fwd = [pltpu.roll(w, 1, 1) for w in panels]
        bwd = [pltpu.roll(w, LANES - 1, 1) for w in panels]
        for j in range(total):
            w = panels[j]
            yield (pltpu.roll(w, 1, 0) + pltpu.roll(w, tall - 1, 0)
                   + jnp.where(first, fwd[(j - 1) % total], fwd[j])
                   + jnp.where(last, bwd[(j + 1) % total], bwd[j]))

    for j, s in enumerate(around([cell_s[j] for j in range(npan + 1)])):
        diag_s[j] = diag_s[j] + cell_s[j] * s - shift

    def dots(a, b, total):
        term = fold(a[:rows] * b[:rows])
        return term if total is None else total + term

    moments = []
    for s in range(2):
        m = [None] * 6
        for step, (src, dst) in enumerate(((v0, v1), (v1, v2), (v2, None))):
            weighted = [cell_s[j] * src[s, j] for j in range(npan + 1)]
            for j, near in enumerate(around(weighted)):
                if dst is None and j == npan:
                    continue
                field = src[s, j]
                image = diag_s[j] * field - cell_s[j] * near
                if dst is not None:
                    dst[s, j] = image
                if j < npan:
                    if step == 0:
                        m[0] = dots(field, field, m[0])
                    m[2 * step + 1] = dots(field, image, m[2 * step + 1])
                    if step < 2:
                        m[2 * step + 2] = dots(image, image, m[2 * step + 2])
        moments.append(m)

    gap = jnp.zeros((2, LANES), jnp.float32)
    spread = [jnp.sum(x, axis=0, keepdims=True) for x in moments[0]] + [gap]
    spread += [jnp.sum(x, axis=0, keepdims=True) for x in moments[1]] + [gap]
    spread = jnp.concatenate(spread, axis=0)
    on = iota((2 * SUB, LANES), 0) == iota((2 * SUB, LANES), 1)
    sums = jnp.sum(spread, axis=1, keepdims=True)
    sums = jnp.sum(jnp.where(on, sums, 0.0), axis=0, keepdims=True)

    base = 0
    for number, stage in enumerate(stages):
        part[number] = sums
        copies = []
        for k in range(1, counts[stage]):
            copies.append(pltpu.make_async_remote_copy(
                src_ref=part.at[number], dst_ref=got_part.at[base + k],
                send_sem=psend_sem.at[base + k], recv_sem=precv_sem.at[base + k],
                device_id=peer(stage, k), device_id_type=MESH))
            copies[-1].start()
        for copy in copies:
            copy.wait_recv()
        for k in range(1, counts[stage]):
            sums = sums + got_part[base + k]
        for copy in copies:
            copy.wait_send()
        base += counts[stage]

    sums = jnp.sum(jnp.where(on, sums, 0.0), axis=1, keepdims=True)
    sums = jnp.broadcast_to(sums, (2 * SUB, LANES))
    stores = []
    for s, out_h in enumerate((out0_h, out1_h)):
        m = [sums[s * SUB + i:s * SUB + i + 1] for i in range(6)]
        e0, e1, e2 = coefficients(m, shift)
        for j in range(npan):
            core = pl.ds(0, rows)
            out_v[s, :, pl.ds(j * LANES, LANES)] = (
                e0 * v0[s, j, core, :] + e1 * v1[s, j, core, :] + e2 * v2[s, j, core, :])
        stores.append(pltpu.make_async_copy(out_v.at[s], out_h, out_sem.at[s]))
        stores[-1].start()
    for k in range(8):
        @pl.when(there[k])
        def _():
            halo(k, False).wait_send()
    for store in stores:
        store.wait()


def body(nrow, ncol, wet_mask, land_class, flood_label, conductance, storage, prior_depth, rainfall):
    rows, cols = storage.shape
    nb, npan = rows // SUB, cols // LANES
    stages = ("both",) if nrow * ncol <= 32 else ("col", "row")
    slots = nrow * ncol if len(stages) == 1 else nrow + ncol
    f32, i32 = jnp.float32, jnp.int32
    tile = (rows, cols)
    padded = (npan + 1, rows + SUB, LANES)
    hbm = pl.BlockSpec(memory_space=pl.ANY)
    return pl.pallas_call(
        functools.partial(kernel, nrow, ncol, stages),
        out_shape=(jax.ShapeDtypeStruct(tile, f32), jax.ShapeDtypeStruct(tile, f32)),
        in_specs=[hbm, hbm, hbm, pl.BlockSpec(memory_space=pltpu.SMEM), hbm, hbm, hbm],
        out_specs=(hbm, hbm),
        scratch_shapes=[
            pltpu.VMEM(tile, i32), pltpu.VMEM(tile, i32), pltpu.VMEM(tile, i32),
            pltpu.VMEM(tile, f32), pltpu.VMEM(tile, f32), pltpu.VMEM(tile, f32),
            pltpu.VMEM((2,) + tile, f32),
            pltpu.VMEM((2,) + padded, f32), pltpu.VMEM((2,) + padded, f32), pltpu.VMEM((2,) + padded, f32),
            pltpu.VMEM(padded, f32), pltpu.VMEM(padded, f32),
            pltpu.VMEM((2, 2, npan, SUB, LANES), f32), pltpu.VMEM((2, SUB, LANES), f32),
            pltpu.VMEM((2, 2, npan, SUB, LANES), f32), pltpu.VMEM((6, SUB, LANES), f32),
            pltpu.VMEM((2, 1, LANES), f32), pltpu.VMEM((slots, 1, LANES), f32),
            pltpu.SemaphoreType.DMA((6,)), pltpu.SemaphoreType.DMA((2,)),
            pltpu.SemaphoreType.DMA((8,)), pltpu.SemaphoreType.DMA((8,)),
            pltpu.SemaphoreType.DMA((slots,)), pltpu.SemaphoreType.DMA((slots,)),
        ],
        compiler_params=pltpu.CompilerParams(
            collective_id=0, has_side_effects=True, vmem_limit_bytes=32 * 1024 * 1024),
        name="moments",
    )(wet_mask, land_class, flood_label, conductance, storage, prior_depth, rainfall)


def solution(mesh):
    spread = P(("basin", "row"), "col")
    return jax.shard_map(
        functools.partial(body, mesh.shape["row"], mesh.shape["col"]),
        mesh=mesh,
        in_specs=(spread, spread, spread, P(), spread, spread, spread),
        out_specs=(spread, spread),
        check_vma=False,
    )
```

time: 229 us -> 24.6 us (0.11)
  blocking collectives: 154 us -> 0 us
  starting transfers between devices: 30.6 us -> 0 us
  waiting for transfers between devices: 23.7 us -> 0 us
  Pallas kernels: 0 us -> 15.9 us
  other arithmetic: 15.9 us -> 0 us
  local copies, waits for them, and re-layouts: 2.85 us -> 7.75 us
    psum x5 -> x0, blocking collectives: 154 us -> none  [the longest x3 91.4 us: squares(): return lax.psum(jnp.sum(residual * residual, axis=(1, 2)), ('row', 'col'))]
    ppermute x16 -> x0, starting transfers between devices: 30.6 us -> none  [the longest x8 20.2 us: extended(): before = lax.ppermute(last, axis, up)]
    ppermute x16 -> x0, waiting for transfers between devices: 23.7 us -> none  [the longest x8 21.4 us: extended(): after = lax.ppermute(initial, axis, down)]
    pallas_call x0 -> x1, Pallas kernels: none -> 15.9 us  [body(): pl.pallas_call(functools.partial(kernel, nrow, ncol, stages), out_shape=(...]
    mul x1 -> x0, other arithmetic: 11.5 us -> none  [cell_values(): return value * wet]
    unnamed x8 -> x16, local copies, waits for them, and re-layouts: 0.03 us -> 7.75 us
  transfers between devices with their start and end apart: 16 -> 0, of which waited for: 8 -> 0; matrix products, arithmetic and copies ran while one was open for 0% -> 0% of each run, Pallas kernels for 0% -> 0%
where the time goes in v1:
time: 24.6 us; the launch traced here: 24.3 us
  Pallas kernels  15.9 us (65%)
  local copies, waits for them, and re-layouts  7.75 us (32%)
  between operations  0.66 us (3%)
    pallas_call x1, Pallas kernels, body(): pl.pallas_call(functools.partial(kernel, nrow, ncol, stages), out_shape=(...  15.9 us
    unnamed x16, local copies, waits for them, and re-layouts  7.75 us

profile of v1, /device:TPU:0, one launch (start us, length us, event | category | flops | bytes accessed | tf_op | source)
XLA Modules:
  0.0 24.3 jit_solution(10572792683638942436)
XLA Ops:
  0.6 0.0 copy-start
  0.6 0.9 %copy-done = s32[64,1024]{1,0:T(8,128)S(1)} copy-done((s32[64,1024]{1,0:T(8,128)S(1)}, s32[64,1024]{1,0:T(8,128)}, u32[]{:S(2)}) %copy-start) | copy-done | bytes 262168
  1.6 0.0 copy-start.1
  1.6 0.9 %copy-done.1 = s32[64,1024]{1,0:T(8,128)S(1)} copy-done((s32[64,1024]{1,0:T(8,128)S(1)}, s32[64,1024]{1,0:T(8,128)}, u32[]{:S(2)}) %copy-start.1) | copy-done | bytes 262168
  2.5 0.0 copy-start.2
  2.5 0.9 %copy-done.2 = s32[64,1024]{1,0:T(8,128)S(1)} copy-done((s32[64,1024]{1,0:T(8,128)S(1)}, s32[64,1024]{1,0:T(8,128)}, u32[]{:S(2)}) %copy-start.2) | copy-done | bytes 262168
  3.5 0.0 copy-start.3
  3.5 0.9 %copy-done.3 = f32[64,1024]{1,0:T(8,128)S(1)} copy-done((f32[64,1024]{1,0:T(8,128)S(1)}, f32[64,1024]{1,0:T(8,128)}, u32[]{:S(2)}) %copy-start.3) | copy-done | bytes 262168
  4.4 0.0 copy-start.4
  4.4 0.9 %copy-done.4 = f32[64,1024]{1,0:T(8,128)S(1)} copy-done((f32[64,1024]{1,0:T(8,128)S(1)}, f32[64,1024]{1,0:T(8,128)}, u32[]{:S(2)}) %copy-start.4) | copy-done | bytes 262168
  5.4 0.0 copy-start.5
  5.4 0.9 %copy-done.5 = f32[64,1024]{1,0:T(8,128)S(1)} copy-done((f32[64,1024]{1,0:T(8,128)S(1)}, f32[64,1024]{1,0:T(8,128)}, u32[]{:S(2)}) %copy-start.5) | copy-done | bytes 262168
  6.3 0.0 copy-start.6
  6.3 0.7 %copy-done.6 = f32[16]{0:T(128)S(1)} copy-done((f32[16]{0:T(128)S(1)}, f32[16]{0:T(128)}, u32[]{:S(2)}) %copy-start.6) | copy-done | bytes 88
  7.0 15.9 %moments.1 = (f32[64,1024]{1,0:T(8,128)S(1)}, f32[64,1024]{1,0:T(8,128)S(1)}) custom-call(s32[64,1024]{1,0:T(8,128)S(1)} %copy-done, s32[64,1024]{1,0:T(8,128)S(1)} %copy-done.1, s32[64,1024]{1,0:T(8,128)S(1)} %copy-done.2, f32[16]{0:T(128)S(1)} %copy-done.6, f32[64,1024]{1,0:T(8,128)S(1)} %copy-done.3, f32[64,1024]{1,0:T(8,128)S(1)} %copy-done.4, ...), custom_call_target="tpu_custom_call" | custom-call | tf_op jit(solution)/shard_map/moments/pallas_call | solution.py:304
  22.9 0.7 %copy.11 = f32[64,1024]{1,0:T(8,128)} copy(f32[64,1024]{1,0:T(8,128)S(1)} %get-tuple-element.4) | data formatting | bytes 524288
  23.6 0.7 %copy.12 = f32[64,1024]{1,0:T(8,128)} copy(f32[64,1024]{1,0:T(8,128)S(1)} %get-tuple-element.5) | data formatting | bytes 524288
Async XLA Ops:
  0.6 1.0 %copy-start = (s32[64,1024]{1,0:T(8,128)S(1)}, s32[64,1024]{1,0:T(8,128)}, u32[]{:S(2)}) copy-start(s32[64,1024]{1,0:T(8,128)} %wet_h.1) | copy-start | bytes 786436
  1.6 0.9 %copy-start.1 = (s32[64,1024]{1,0:T(8,128)S(1)}, s32[64,1024]{1,0:T(8,128)}, u32[]{:S(2)}) copy-start(s32[64,1024]{1,0:T(8,128)} %land_h.1) | copy-start | bytes 786436
  2.5 0.9 %copy-start.2 = (s32[64,1024]{1,0:T(8,128)S(1)}, s32[64,1024]{1,0:T(8,128)}, u32[]{:S(2)}) copy-start(s32[64,1024]{1,0:T(8,128)} %label_h.1) | copy-start | bytes 786436
  3.5 0.9 %copy-start.3 = (f32[64,1024]{1,0:T(8,128)S(1)}, f32[64,1024]{1,0:T(8,128)}, u32[]{:S(2)}) copy-start(f32[64,1024]{1,0:T(8,128)} %stor_h.1) | copy-start | bytes 786436
  4.4 0.9 %copy-start.4 = (f32[64,1024]{1,0:T(8,128)S(1)}, f32[64,1024]{1,0:T(8,128)}, u32[]{:S(2)}) copy-start(f32[64,1024]{1,0:T(8,128)} %prior_h.1) | copy-start | bytes 786436
  5.4 0.9 %copy-start.5 = (f32[64,1024]{1,0:T(8,128)S(1)}, f32[64,1024]{1,0:T(8,128)}, u32[]{:S(2)}) copy-start(f32[64,1024]{1,0:T(8,128)} %rain_h.1) | copy-start | bytes 786436
  6.3 0.7 %copy-start.6 = (f32[16]{0:T(128)S(1)}, f32[16]{0:T(128)}, u32[]{:S(2)}) copy-start(f32[16]{0:T(128)} %cond.1) | copy-start | bytes 196

commit v2 on v1

--- a/solution.py
+++ b/solution.py
@@ -11,6 +11,7 @@
 LANES = 128
 SUB = 8
 PIECE = 4
+LIMIT = 63500 * 1024
 STEPS = (
     (-1, 0), (1, 0), (0, -1), (0, 1), (-1, -1), (-1, 1), (1, -1), (1, 1),
 )
@@ -58,8 +59,8 @@
 
 def kernel(
     nrow, ncol, stages,
-    wet_h, land_h, label_h, cond, stor_h, prior_h, rain_h, out0_h, out1_h,
-    wet_v, land_v, label_v, stor_v, prior_v, rain_v, out_v,
+    wet_h, land_h, label_h, cond_h, stor_h, prior_h, rain_h, out0_h, out1_h,
+    wet_v, land_v, label_v, stor_v, prior_v, rain_v, cond, out_v,
     v0, v1, v2, cell_s, diag_s,
     pack_rows, pack_cols, got_rows, got_cols, part, got_part,
     in_sem, out_sem, send_sem, recv_sem, psend_sem, precv_sem,
@@ -72,7 +73,7 @@
         pltpu.make_async_copy(src, dst, in_sem.at[i])
         for i, (src, dst) in enumerate((
             (land_h, land_v), (wet_h, wet_v), (stor_h, stor_v),
-            (prior_h, prior_v), (rain_h, rain_v), (label_h, label_v)))
+            (prior_h, prior_v), (rain_h, rain_v), (label_h, label_v), (cond_h, cond)))
     ]
     for load in loads:
         load.start()
@@ -115,14 +116,14 @@
                 pl.semaphore_signal(barrier, inc=1, device_id=place(k), device_id_type=MESH)
             expect = expect + there[k].astype(jnp.int32)
 
+    for load in loads:
+        load.wait()
     shift = cond[0]
     for i in range(1, cond.shape[0]):
         shift = shift + cond[i]
     shift = shift * (2.0 / cond.shape[0])
     shift = shift * shift
 
-    for load in loads:
-        load.wait()
     for j in range(npan):
         at = pl.ds(j * LANES, LANES)
         wet = wet_v[:, at].astype(jnp.float32)
@@ -278,16 +279,33 @@
     for s, out_h in enumerate((out0_h, out1_h)):
         m = [sums[s * SUB + i:s * SUB + i + 1] for i in range(6)]
         e0, e1, e2 = coefficients(m, shift)
-        for j in range(npan):
-            core = pl.ds(0, rows)
-            out_v[s, :, pl.ds(j * LANES, LANES)] = (
-                e0 * v0[s, j, core, :] + e1 * v1[s, j, core, :] + e2 * v2[s, j, core, :])
-        stores.append(pltpu.make_async_copy(out_v.at[s], out_h, out_sem.at[s]))
-        stores[-1].start()
+        for half in range(2):
+            low = half * (rows // 2)
+            core = pl.ds(low, rows // 2)
+            for j in range(npan):
+                out_v[s, core, pl.ds(j * LANES, LANES)] = (
+                    e0 * v0[s, j, core, :] + e1 * v1[s, j, core, :] + e2 * v2[s, j, core, :])
+            stores.append(pltpu.make_async_copy(out_v.at[s, core], out_h.at[core], out_sem.at[2 * s + half]))
+            stores[-1].start()
     for k in range(8):
         @pl.when(there[k])
         def _():
             halo(k, False).wait_send()
+    for store in stores:
+        store.wait()
+
+
+def hand_over(a_h, b_h, out0_h, out1_h, held, sem, out_sem):
+    loads, stores = [], []
+    for s, (src, dst) in enumerate(((a_h, out0_h), (b_h, out1_h))):
+        for h in range(2):
+            at = pl.ds(h * (src.shape[0] // 2), src.shape[0] // 2)
+            loads.append(pltpu.make_async_copy(src.at[at], held.at[s, at], sem.at[s, h]))
+            stores.append(pltpu.make_async_copy(held.at[s, at], dst.at[at], out_sem.at[s, h]))
+            loads[-1].start()
+    for load, store in zip(loads, stores):
+        load.wait()
+        store.start()
     for store in stores:
         store.wait()
 
@@ -299,30 +317,41 @@
     slots = nrow * ncol if len(stages) == 1 else nrow + ncol
     f32, i32 = jnp.float32, jnp.int32
     tile = (rows, cols)
+    table = conductance.shape[0]
     padded = (npan + 1, rows + SUB, LANES)
-    hbm = pl.BlockSpec(memory_space=pl.ANY)
-    return pl.pallas_call(
+    hbm = pl.BlockSpec(memory_space=pltpu.HBM)
+    near = pl.BlockSpec(memory_space=pl.ANY)
+    outs = pl.pallas_call(
         functools.partial(kernel, nrow, ncol, stages),
         out_shape=(jax.ShapeDtypeStruct(tile, f32), jax.ShapeDtypeStruct(tile, f32)),
-        in_specs=[hbm, hbm, hbm, pl.BlockSpec(memory_space=pltpu.SMEM), hbm, hbm, hbm],
-        out_specs=(hbm, hbm),
+        in_specs=[hbm] * 7,
+        out_specs=(near, near),
         scratch_shapes=[
             pltpu.VMEM(tile, i32), pltpu.VMEM(tile, i32), pltpu.VMEM(tile, i32),
             pltpu.VMEM(tile, f32), pltpu.VMEM(tile, f32), pltpu.VMEM(tile, f32),
-            pltpu.VMEM((2,) + tile, f32),
+            pltpu.SMEM((table,), f32), pltpu.VMEM((2,) + tile, f32),
             pltpu.VMEM((2,) + padded, f32), pltpu.VMEM((2,) + padded, f32), pltpu.VMEM((2,) + padded, f32),
             pltpu.VMEM(padded, f32), pltpu.VMEM(padded, f32),
             pltpu.VMEM((2, 2, npan, SUB, LANES), f32), pltpu.VMEM((2, SUB, LANES), f32),
             pltpu.VMEM((2, 2, npan, SUB, LANES), f32), pltpu.VMEM((6, SUB, LANES), f32),
             pltpu.VMEM((2, 1, LANES), f32), pltpu.VMEM((slots, 1, LANES), f32),
-            pltpu.SemaphoreType.DMA((6,)), pltpu.SemaphoreType.DMA((2,)),
+            pltpu.SemaphoreType.DMA((7,)), pltpu.SemaphoreType.DMA((4,)),
             pltpu.SemaphoreType.DMA((8,)), pltpu.SemaphoreType.DMA((8,)),
             pltpu.SemaphoreType.DMA((slots,)), pltpu.SemaphoreType.DMA((slots,)),
         ],
         compiler_params=pltpu.CompilerParams(
-            collective_id=0, has_side_effects=True, vmem_limit_bytes=32 * 1024 * 1024),
+            collective_id=0, has_side_effects=True, vmem_limit_bytes=LIMIT),
         name="moments",
     )(wet_mask, land_class, flood_label, conductance, storage, prior_depth, rainfall)
+    return pl.pallas_call(
+        hand_over,
+        out_shape=(jax.ShapeDtypeStruct(tile, f32), jax.ShapeDtypeStruct(tile, f32)),
+        in_specs=[near, near],
+        out_specs=(near, near),
+        scratch_shapes=[pltpu.VMEM((2,) + tile, f32), pltpu.SemaphoreType.DMA((2, 2)), pltpu.SemaphoreType.DMA((2, 2))],
+        compiler_params=pltpu.CompilerParams(vmem_limit_bytes=LIMIT),
+        name="hand_over",
+    )(*outs)
 
 
 def solution(mesh):

time: 24.6 us -> 18.5 us (0.75)
  local copies, waits for them, and re-layouts: 7.75 us -> 0 us
  Pallas kernels: 15.9 us -> 17.7 us
    unnamed x16 -> x0, local copies, waits for them, and re-layouts: 7.75 us -> none
    pallas_call x0 -> x1, Pallas kernels: none -> 1.82 us  [body(): pl.pallas_call(hand_over, out_shape=(jax.ShapeDtypeStruct(tile, f32), jax...]
where the time goes in v2:
time: 18.5 us; the launch traced here: 18.3 us
  Pallas kernels  17.7 us (96%)
  between operations  0.64 us (3%)
    pallas_call x1, Pallas kernels, body(): pl.pallas_call(functools.partial(kernel, nrow, ncol, stages), out_shape=(...  15.9 us
    pallas_call x1, Pallas kernels, body(): pl.pallas_call(hand_over, out_shape=(jax.ShapeDtypeStruct(tile, f32), jax...  1.82 us

profile of v2, /device:TPU:0, one launch (start us, length us, event | category | flops | bytes accessed | tf_op | source)
XLA Modules:
  0.0 18.3 jit_solution(14438379136684653927)
XLA Ops:
  0.6 15.9 %moments.1 = (f32[64,1024]{1,0:T(8,128)}, f32[64,1024]{1,0:T(8,128)}) custom-call(s32[64,1024]{1,0:T(8,128)} %wet_h.1, s32[64,1024]{1,0:T(8,128)} %land_h.1, s32[64,1024]{1,0:T(8,128)} %label_h.1, f32[16]{0:T(128)} %cond_h.1, f32[64,1024]{1,0:T(8,128)} %stor_h.1, f32[64,1024]{1,0:T(8,128)} %prior_h.1, f32[64,1024]{1,0:T(8,128)} %rain_h.1), custom_call_target="tpu_custom_call" | custom-call | tf_op jit(solution)/shard_map/moments/pallas_call | solution.py:324
  16.5 1.8 %hand_over.1 = (f32[64,1024]{1,0:T(8,128)}, f32[64,1024]{1,0:T(8,128)}) custom-call(f32[64,1024]{1,0:T(8,128)} %get-tuple-element.4.a_h, f32[64,1024]{1,0:T(8,128)} %get-tuple-element.5.b_h), custom_call_target="tpu_custom_call" | custom-call | tf_op jit(solution)/shard_map/hand_over/pallas_call | solution.py:346

commit v3 on v2

--- a/solution.py
+++ b/solution.py
@@ -61,7 +61,7 @@
     nrow, ncol, stages,
     wet_h, land_h, label_h, cond_h, stor_h, prior_h, rain_h, out0_h, out1_h,
     wet_v, land_v, label_v, stor_v, prior_v, rain_v, cond, out_v,
-    v0, v1, v2, cell_s, diag_s,
+    v0, v1, v2, cell_s, diag_s, diag_in,
     pack_rows, pack_cols, got_rows, got_cols, part, got_part,
     in_sem, out_sem, send_sem, recv_sem, psend_sem, precv_sem,
 ):
@@ -179,6 +179,51 @@
         @pl.when(there[k])
         def _():
             halo(k, False).start()
+    def around(panels):
+        tall, total = panels[0].shape[0], len(panels)
+        first = iota((tall, LANES), 1) == 0
+        last = iota((tall, LANES), 1) == LANES - 1
+        fwd = [pltpu.roll(w, 1, 1) for w in panels]
+        bwd = [pltpu.roll(w, LANES - 1, 1) for w in panels]
+        return [
+            pltpu.roll(w, 1, 0) + pltpu.roll(w, tall - 1, 0)
+            + jnp.where(first, fwd[(j - 1) % total], fwd[j])
+            + jnp.where(last, bwd[(j + 1) % total], bwd[j])
+            for j, w in enumerate(panels)
+        ]
+
+    def dots(a, b, total):
+        term = fold(a * b)
+        return term if total is None else total + term
+
+    def gather(m, step, field, image):
+        if step == 0:
+            m[0] = dots(field, field, m[0])
+        m[2 * step + 1] = dots(field, image, m[2 * step + 1])
+        if step < 2:
+            m[2 * step + 2] = dots(image, image, m[2 * step + 2])
+
+    whole = pl.ds(0, rows)
+    middle = pl.ds(SUB, rows - 2 * SUB)
+    inside = slice(SUB, rows - SUB)
+    nears = around([cell_s[j, whole, :] for j in range(npan)])
+    for j in range(npan):
+        diag_in[j] = diag_s[j, whole, :] + cell_s[j, whole, :] * nears[j] - shift
+    moments = [[None] * 6, [None] * 6]
+    for s in range(2):
+        for step, (src, dst) in enumerate(((v0, v1), (v1, v2), (v2, None))):
+            nears = around([cell_s[j, whole, :] * src[s, j, whole, :] for j in range(npan)])
+            for j in range(npan):
+                deep = 0 < j < npan - 1
+                if dst is None and not deep:
+                    continue
+                field = src[s, j, whole, :]
+                image = diag_in[j] * field - cell_s[j, whole, :] * nears[j]
+                if dst is not None:
+                    dst[s, j, whole, :] = image
+                if deep:
+                    gather(moments[s], step, field[inside], image[inside])
+
     for k in range(8):
         @pl.when(there[k])
         def _():
@@ -206,46 +251,53 @@
         field[npan, tail, :] = jnp.where(
             upper, side(got_cols[5], got_cols[4], 0), side(got_cols[3], got_cols[2], nb - 1))
 
-    tall = rows + SUB
-    first = iota((tall, LANES), 1) == 0
-    last = iota((tall, LANES), 1) == LANES - 1
-
-    def around(panels):
-        total = npan + 1
-        fwd = [pltpu.roll(w, 1, 1) for w in panels]
-        bwd = [pltpu.roll(w, LANES - 1, 1) for w in panels]
-        for j in range(total):
-            w = panels[j]
-            yield (pltpu.roll(w, 1, 0) + pltpu.roll(w, tall - 1, 0)
-                   + jnp.where(first, fwd[(j - 1) % total], fwd[j])
-                   + jnp.where(last, bwd[(j + 1) % total], bwd[j]))
-
-    for j, s in enumerate(around([cell_s[j] for j in range(npan + 1)])):
-        diag_s[j] = diag_s[j] + cell_s[j] * s - shift
-
-    def dots(a, b, total):
-        term = fold(a[:rows] * b[:rows])
-        return term if total is None else total + term
-
-    moments = []
+    ring = [npan - 2, npan - 1, npan, 0, 1]
+
+    def wide(field, j):
+        return jnp.concatenate(
+            [field[j, pl.ds(rows - 2 * SUB, 3 * SUB), :], field[j, pl.ds(0, 2 * SUB), :]], axis=0)
+
+    def narrow(field, j):
+        return jnp.concatenate(
+            [field[j, pl.ds(rows - SUB, 2 * SUB), :], field[j, pl.ds(0, SUB), :]], axis=0)
+
+    def put(field, j, value):
+        field[j, pl.ds(rows - SUB, 2 * SUB), :] = value[:2 * SUB]
+        field[j, pl.ds(0, SUB), :] = value[2 * SUB:]
+
+    def ends(value):
+        return jnp.concatenate([value[:SUB], value[2 * SUB:]], axis=0)
+
+    nears = around([wide(cell_s, j) for j in range(npan + 1)])
+    for j in range(npan + 1):
+        value = narrow(diag_s, j) + narrow(cell_s, j) * nears[j][SUB:4 * SUB] - shift
+        put(diag_s, j, value)
+    nears = around([cell_s[j, whole, :] for j in ring])
+    for j, near in zip(ring[1:4], nears[1:4]):
+        diag_s[j, middle, :] = diag_s[j, middle, :] + cell_s[j, middle, :] * near[SUB:rows - SUB] - shift
     for s in range(2):
-        m = [None] * 6
+        m = moments[s]
         for step, (src, dst) in enumerate(((v0, v1), (v1, v2), (v2, None))):
-            weighted = [cell_s[j] * src[s, j] for j in range(npan + 1)]
-            for j, near in enumerate(around(weighted)):
+            nears = around([wide(cell_s, j) * wide(src.at[s], j) for j in range(npan + 1)])
+            for j in range(npan + 1):
                 if dst is None and j == npan:
                     continue
-                field = src[s, j]
-                image = diag_s[j] * field - cell_s[j] * near
+                field = narrow(src.at[s], j)
+                image = narrow(diag_s, j) * field - narrow(cell_s, j) * nears[j][SUB:4 * SUB]
                 if dst is not None:
-                    dst[s, j] = image
+                    put(dst.at[s], j, image)
                 if j < npan:
-                    if step == 0:
-                        m[0] = dots(field, field, m[0])
-                    m[2 * step + 1] = dots(field, image, m[2 * step + 1])
-                    if step < 2:
-                        m[2 * step + 2] = dots(image, image, m[2 * step + 2])
-        moments.append(m)
+                    gather(m, step, ends(field), ends(image))
+            nears = around([cell_s[j, whole, :] * src[s, j, whole, :] for j in ring])
+            for j, near in zip(ring[1:4], nears[1:4]):
+                if dst is None and j == npan:
+                    continue
+                field = src[s, j, middle, :]
+                image = diag_s[j, middle, :] * field - cell_s[j, middle, :] * near[SUB:rows - SUB]
+                if dst is not None:
+                    dst[s, j, middle, :] = image
+                if j < npan:
+                    gather(m, step, field, image)
 
     gap = jnp.zeros((2, LANES), jnp.float32)
     spread = [jnp.sum(x, axis=0, keepdims=True) for x in moments[0]] + [gap]
@@ -331,7 +383,7 @@
             pltpu.VMEM(tile, f32), pltpu.VMEM(tile, f32), pltpu.VMEM(tile, f32),
             pltpu.SMEM((table,), f32), pltpu.VMEM((2,) + tile, f32),
             pltpu.VMEM((2,) + padded, f32), pltpu.VMEM((2,) + padded, f32), pltpu.VMEM((2,) + padded, f32),
-            pltpu.VMEM(padded, f32), pltpu.VMEM(padded, f32),
+            pltpu.VMEM(padded, f32), pltpu.VMEM(padded, f32), pltpu.VMEM((npan, rows, LANES), f32),
             pltpu.VMEM((2, 2, npan, SUB, LANES), f32), pltpu.VMEM((2, SUB, LANES), f32),
             pltpu.VMEM((2, 2, npan, SUB, LANES), f32), pltpu.VMEM((6, SUB, LANES), f32),
             pltpu.VMEM((2, 1, LANES), f32), pltpu.VMEM((slots, 1, LANES), f32),

time: 18.5 us -> 17.9 us (0.968)
  Pallas kernels: 17.7 us -> 17.1 us
    pallas_call x1, Pallas kernels: 15.9 us -> 15.3 us  [body(): pl.pallas_call(functools.partial(kernel, nrow, ncol, stages), out_shape=(...]
where the time goes in v3:
time: 17.9 us; the launch traced here: 17.7 us
  Pallas kernels  17.1 us (96%)
  between operations  0.64 us (4%)
    pallas_call x1, Pallas kernels, body(): pl.pallas_call(functools.partial(kernel, nrow, ncol, stages), out_shape=(...  15.3 us
    pallas_call x1, Pallas kernels, body(): pl.pallas_call(hand_over, out_shape=(jax.ShapeDtypeStruct(tile, f32), jax...  1.82 us

profile of v3, /device:TPU:0, one launch (start us, length us, event | category | flops | bytes accessed | tf_op | source)
XLA Modules:
  0.0 17.7 jit_solution(2132004473207182596)
XLA Ops:
  0.6 15.3 %moments.1 = (f32[64,1024]{1,0:T(8,128)}, f32[64,1024]{1,0:T(8,128)}) custom-call(s32[64,1024]{1,0:T(8,128)} %wet_h.1, s32[64,1024]{1,0:T(8,128)} %land_h.1, s32[64,1024]{1,0:T(8,128)} %label_h.1, f32[16]{0:T(128)} %cond_h.1, f32[64,1024]{1,0:T(8,128)} %stor_h.1, f32[64,1024]{1,0:T(8,128)} %prior_h.1, f32[64,1024]{1,0:T(8,128)} %rain_h.1), custom_call_target="tpu_custom_call" | custom-call | tf_op jit(solution)/shard_map/moments/pallas_call | solution.py:376
  15.9 1.8 %hand_over.1 = (f32[64,1024]{1,0:T(8,128)}, f32[64,1024]{1,0:T(8,128)}) custom-call(f32[64,1024]{1,0:T(8,128)} %get-tuple-element.4.a_h, f32[64,1024]{1,0:T(8,128)} %get-tuple-element.5.b_h), custom_call_target="tpu_custom_call" | custom-call | tf_op jit(solution)/shard_map/hand_over/pallas_call | solution.py:398

commit v4 on v3

--- a/solution.py
+++ b/solution.py
@@ -124,16 +124,24 @@
     shift = shift * (2.0 / cond.shape[0])
     shift = shift * shift
 
+
+    def prepare(j, low, count):
+        at = pl.ds(j * LANES, LANES)
+        core = pl.ds(low, count)
+        wet = wet_v[core, at].astype(jnp.float32)
+        prior = prior_v[core, at]
+        stor = stor_v[core, at]
+        cell_s[j, core, :] = lookup(land_v[core, at], cond) * wet
+        v0[0, j, core, :] = stor * prior + wet * rain_v[core, at]
+        v0[1, j, core, :] = wet * (1.0 / (1.0 + jnp.exp(-prior)) - label_v[core, at].astype(jnp.float32))
+        diag_s[j, core, :] = stor
+
     for j in range(npan):
-        at = pl.ds(j * LANES, LANES)
-        wet = wet_v[:, at].astype(jnp.float32)
-        prior = prior_v[:, at]
-        stor = stor_v[:, at]
-        core = pl.ds(0, rows)
-        cell_s[j, core, :] = lookup(land_v[:, at], cond) * wet
-        v0[0, j, core, :] = stor * prior + wet * rain_v[:, at]
-        v0[1, j, core, :] = wet * (1.0 / (1.0 + jnp.exp(-prior)) - label_v[:, at].astype(jnp.float32))
-        diag_s[j, core, :] = stor
+        if 0 < j < npan - 1:
+            prepare(j, 0, SUB)
+            prepare(j, rows - SUB, SUB)
+        else:
+            prepare(j, 0, rows)
 
     fields = (v0.at[0], v0.at[1], cell_s, diag_s)
     sub = iota((SUB, LANES), 0)
@@ -179,6 +187,9 @@
         @pl.when(there[k])
         def _():
             halo(k, False).start()
+    for j in range(1, npan - 1):
+        prepare(j, SUB, rows - 2 * SUB)
+
     def around(panels):
         tall, total = panels[0].shape[0], len(panels)
         first = iota((tall, LANES), 1) == 0

time: 17.9 us -> 17.9 us (level)
  no operation moved by 1% of the time
where the time goes in v4:
time: 17.9 us; the launch traced here: 17.7 us
  Pallas kernels  17.1 us (96%)
  between operations  0.64 us (4%)
    pallas_call x1, Pallas kernels, body(): pl.pallas_call(functools.partial(kernel, nrow, ncol, stages), out_shape=(...  15.3 us
    pallas_call x1, Pallas kernels, body(): pl.pallas_call(hand_over, out_shape=(jax.ShapeDtypeStruct(tile, f32), jax...  1.82 us

profile of v4, /device:TPU:0, one launch (start us, length us, event | category | flops | bytes accessed | tf_op | source)
XLA Modules:
  0.0 17.7 jit_solution(1646398079435558645)
XLA Ops:
  0.6 15.3 %moments.1 = (f32[64,1024]{1,0:T(8,128)}, f32[64,1024]{1,0:T(8,128)}) custom-call(s32[64,1024]{1,0:T(8,128)} %wet_h.1, s32[64,1024]{1,0:T(8,128)} %land_h.1, s32[64,1024]{1,0:T(8,128)} %label_h.1, f32[16]{0:T(128)} %cond_h.1, f32[64,1024]{1,0:T(8,128)} %stor_h.1, f32[64,1024]{1,0:T(8,128)} %prior_h.1, f32[64,1024]{1,0:T(8,128)} %rain_h.1), custom_call_target="tpu_custom_call" | custom-call | tf_op jit(solution)/shard_map/moments/pallas_call | solution.py:387
  15.9 1.8 %hand_over.1 = (f32[64,1024]{1,0:T(8,128)}, f32[64,1024]{1,0:T(8,128)}) custom-call(f32[64,1024]{1,0:T(8,128)} %get-tuple-element.4.a_h, f32[64,1024]{1,0:T(8,128)} %get-tuple-element.5.b_h), custom_call_target="tpu_custom_call" | custom-call | tf_op jit(solution)/shard_map/hand_over/pallas_call | solution.py:409

commit v5 on v3

--- a/solution.py
+++ b/solution.py
@@ -350,8 +350,8 @@
 def hand_over(a_h, b_h, out0_h, out1_h, held, sem, out_sem):
     loads, stores = [], []
     for s, (src, dst) in enumerate(((a_h, out0_h), (b_h, out1_h))):
-        for h in range(2):
-            at = pl.ds(h * (src.shape[0] // 2), src.shape[0] // 2)
+        for h in range(4):
+            at = pl.ds(h * (src.shape[0] // 4), src.shape[0] // 4)
             loads.append(pltpu.make_async_copy(src.at[at], held.at[s, at], sem.at[s, h]))
             stores.append(pltpu.make_async_copy(held.at[s, at], dst.at[at], out_sem.at[s, h]))
             loads[-1].start()
@@ -400,7 +400,7 @@
         out_shape=(jax.ShapeDtypeStruct(tile, f32), jax.ShapeDtypeStruct(tile, f32)),
         in_specs=[near, near],
         out_specs=(near, near),
-        scratch_shapes=[pltpu.VMEM((2,) + tile, f32), pltpu.SemaphoreType.DMA((2, 2)), pltpu.SemaphoreType.DMA((2, 2))],
+        scratch_shapes=[pltpu.VMEM((2,) + tile, f32), pltpu.SemaphoreType.DMA((2, 4)), pltpu.SemaphoreType.DMA((2, 4))],
         compiler_params=pltpu.CompilerParams(vmem_limit_bytes=LIMIT),
         name="hand_over",
     )(*outs)

time: 17.9 us -> 18 us (level)
  no operation moved by 1% of the time
where the time goes in v5:
time: 18 us; the launch traced here: 17.8 us
  Pallas kernels  17.1 us (95%)
  between operations  0.64 us (4%)
    pallas_call x1, Pallas kernels, body(): pl.pallas_call(functools.partial(kernel, nrow, ncol, stages), out_shape=(...  15.3 us
    pallas_call x1, Pallas kernels, body(): pl.pallas_call(hand_over, out_shape=(jax.ShapeDtypeStruct(tile, f32), jax...  1.83 us

profile of v5, /device:TPU:0, one launch (start us, length us, event | category | flops | bytes accessed | tf_op | source)
XLA Modules:
  0.0 17.8 jit_solution(9416652305508172981)
XLA Ops:
  0.6 15.3 %moments.1 = (f32[64,1024]{1,0:T(8,128)}, f32[64,1024]{1,0:T(8,128)}) custom-call(s32[64,1024]{1,0:T(8,128)} %wet_h.1, s32[64,1024]{1,0:T(8,128)} %land_h.1, s32[64,1024]{1,0:T(8,128)} %label_h.1, f32[16]{0:T(128)} %cond_h.1, f32[64,1024]{1,0:T(8,128)} %stor_h.1, f32[64,1024]{1,0:T(8,128)} %prior_h.1, f32[64,1024]{1,0:T(8,128)} %rain_h.1), custom_call_target="tpu_custom_call" | custom-call | tf_op jit(solution)/shard_map/moments/pallas_call | solution.py:376
  15.9 1.8 %hand_over.1 = (f32[64,1024]{1,0:T(8,128)}, f32[64,1024]{1,0:T(8,128)}) custom-call(f32[64,1024]{1,0:T(8,128)} %get-tuple-element.4.a_h, f32[64,1024]{1,0:T(8,128)} %get-tuple-element.5.b_h), custom_call_target="tpu_custom_call" | custom-call | tf_op jit(solution)/shard_map/hand_over/pallas_call | solution.py:398
